TPU v7x, 256 devices: a whole 4x4x8 slice. The times are simulated.
256 devices in a mesh: dp: 32 (over z_lo, x, core), tp: 8 (over z_hi, y).
Axes of the slice: x: 4, y: 4, z: 8 (z_hi: 2, z_lo: 4; z = z_hi * 4 + z_lo), core: 2. Of those that a mesh axis runs over, the one named last changes fastest.
Arguments:
- tokens: bfloat16 [6144, 3584], P('dp', 'tp'), may hold values from -6 to 6
- cotangent: bfloat16 [6144, 3584], P('dp', 'tp'), may hold values from -6 to 6
- working: bfloat16 [32, 8, 3, 384, 3584], P('dp', 'tp'), may hold values from -0.09375 to 0.09375
- degraded: int32 [32], P('dp'), may hold values from 0 to 1, as said below
- block_map: int32 [32, 16], P('dp'), may hold values from 0 to 7, as said below
- master: float32 [3, 2048, 3584], P(None, ('tp', 'dp')), may hold values from -6 to 6
- moment_one: float32 [3, 2048, 3584], P(None, ('tp', 'dp')), may hold values from -6 to 6
- moment_two: float32 [3, 2048, 3584], P(None, ('tp', 'dp')), may hold values from 0.5 to 8
Outputs:
- input_grad: bfloat16 [6144, 3584], P('dp', 'tp')
- master_next: float32 [3, 2048, 3584], P(None, ('tp', 'dp'))
- moment_one_next: float32 [3, 2048, 3584], P(None, ('tp', 'dp'))
- moment_two_next: float32 [3, 2048, 3584], P(None, ('tp', 'dp'))
Inputs may be any that keep to these rules, and one draw needn't show every extreme that they name: `degraded`: exactly 8 replicas have the value 1. `block_map`: in every row the 16 blocks lie on 6 distinct devices, each of which holds 2 or 3 of them, and at least one holds 3. A row is read only where degraded is 1.
All inputs are finite; a program needn't handle non-finite values.
Results may differ from a plain program's by a relative error of at most 0.0075.
Values may be sent and summed in bfloat16 or wider, within the bound.
A program may use at most 64 MiB of HBM per device.

v0:
```python
import jax
import jax.numpy as jnp
from jax import lax
from jax.sharding import PartitionSpec as P

BLOCK = 128
BLOCKS = 16


beta_one = 0.9
beta_two = 0.95
learn_rate = 0.05
decay_rate = 0.1
adam_eps = 1e-08
bias_one = 1.0 - 0.9**10
bias_two = 1.0 - 0.95**10


def layout_places(replica_flag, mapping, tp_size, slot_count):
    blocks = jnp.arange(BLOCKS, dtype=jnp.int32)
    canonical = blocks // (BLOCKS // tp_size)
    holder = jnp.where(replica_flag > 0, mapping, canonical)
    earlier = (holder[None, :] == holder[:, None]) & (blocks[None, :] < blocks[:, None])
    slot_rank = jnp.sum(earlier.astype(jnp.int32), axis=1)
    return holder * slot_count + slot_rank


def per_device(tokens, cotangent, working, degraded, block_map, master, moment_one, moment_two):
    tp_size = lax.axis_size("tp")
    replicas = lax.axis_size("dp")
    my_index = lax.axis_index("tp")
    weights = working[0, 0]
    slot_count = weights.shape[1] // BLOCK
    per_dev = BLOCKS // tp_size
    places = layout_places(degraded[0], block_map[0], tp_size, slot_count)
    my_slots = my_index * slot_count + jnp.arange(slot_count, dtype=jnp.int32)
    holding = places[:, None] == my_slots[None, :]
    filled = jnp.any(holding, axis=0).astype(jnp.float32)
    column_mask = jnp.repeat(filled, BLOCK)
    inputs, upstream = (
        lax.all_gather(tokens, "tp", axis=1, tiled=True),
        lax.all_gather(cotangent, "tp", axis=1, tiled=True),
    )
    contract_d = (((1,), (1,)), ((), ()))
    gate_pre = lax.dot_general(inputs, weights[0], contract_d, preferred_element_type=jnp.float32)
    up_pre = lax.dot_general(inputs, weights[1], contract_d, preferred_element_type=jnp.float32)
    hidden_grad = lax.dot_general(
        upstream, weights[2], contract_d, preferred_element_type=jnp.float32
    )
    gate_sig = jax.nn.sigmoid(gate_pre)
    active = gate_pre * gate_sig
    hidden = (active * up_pre * column_mask).astype(jnp.bfloat16)
    gate_grad = (
        hidden_grad * up_pre * gate_sig * (1.0 + gate_pre * (1.0 - gate_sig)) * column_mask
    ).astype(jnp.bfloat16)
    up_grad = (hidden_grad * active * column_mask).astype(jnp.bfloat16)
    partial_value = jnp.dot(gate_grad, weights[0], preferred_element_type=jnp.float32) + jnp.dot(
        up_grad, weights[1], preferred_element_type=jnp.float32
    )
    input_grad = lax.psum_scatter(partial_value, "tp", scatter_dimension=1, tiled=True).astype(
        jnp.bfloat16
    )
    tok_rows = gate_grad.shape[0]
    packed = jnp.stack(
        [
            hidden.reshape(tok_rows, slot_count, BLOCK),
            gate_grad.reshape(tok_rows, slot_count, BLOCK),
            up_grad.reshape(tok_rows, slot_count, BLOCK),
        ],
        axis=2,
    )
    packed = packed.transpose(1, 0, 2, 3).reshape(slot_count, tok_rows, 3 * BLOCK)
    wanted = lax.dynamic_slice_in_dim(places, my_index * per_dev, per_dev)
    shard_piece = lax.all_gather(packed, "tp", axis=0, tiled=True)
    positions = jnp.arange(shard_piece.shape[0], dtype=jnp.int32)
    selector = (wanted[:, None] == positions[None, :]).astype(jnp.bfloat16)
    owned_acts = jnp.einsum(
        "kn,ntc->ktc", selector, shard_piece, preferred_element_type=jnp.float32
    ).astype(jnp.bfloat16)
    owned_kinds = (
        owned_acts.reshape(per_dev, tok_rows, 3, BLOCK)
        .transpose(2, 1, 0, 3)
        .reshape(3, tok_rows, per_dev * BLOCK)
    )
    contract_t = (((0,), (0,)), ((), ()))
    gate_term = lax.dot_general(
        owned_kinds[1], inputs, contract_t, preferred_element_type=jnp.float32
    )
    up_term = lax.dot_general(
        owned_kinds[2], inputs, contract_t, preferred_element_type=jnp.float32
    )
    down_term = lax.dot_general(
        owned_kinds[0], upstream, contract_t, preferred_element_type=jnp.float32
    )
    summed = lax.psum_scatter(
        jnp.stack([gate_term, up_term, down_term], axis=1).astype(jnp.bfloat16),
        "dp",
        scatter_dimension=0,
        tiled=True,
    ).astype(jnp.float32)
    grad_mean = jnp.transpose(summed, (1, 0, 2)) / replicas
    moment_one_next = beta_one * moment_one + (1.0 - beta_one) * grad_mean
    moment_two_next = beta_two * moment_two + (1.0 - beta_two) * grad_mean * grad_mean
    update = (
        moment_one_next / bias_one / (jnp.sqrt(moment_two_next / bias_two) + adam_eps)
        + decay_rate * master
    )
    master_next = master - learn_rate * update
    return (input_grad, master_next, moment_one_next, moment_two_next)


def solution(mesh):
    return jax.shard_map(
        per_device,
        mesh=mesh,
        in_specs=(
            P("dp", "tp"),
            P("dp", "tp"),
            P("dp", "tp", None, None, None),
            P("dp"),
            P("dp", None),
            P(None, ("tp", "dp"), None),
            P(None, ("tp", "dp"), None),
            P(None, ("tp", "dp"), None),
        ),
        out_specs=(
            P("dp", "tp"),
            P(None, ("tp", "dp"), None),
            P(None, ("tp", "dp"), None),
            P(None, ("tp", "dp"), None),
        ),
        check_vma=False,
    )
```

profile of v0, /device:TPU:25, one launch (start us, length us, event | category | flops | bytes accessed | tf_op | source)
XLA Modules:
  0.0 533.0 jit_solution(16597101864245584908)
XLA Ops:
  7.2 0.0 all-gather.10.cloned.1.call-start
  7.2 0.7 all-gather.10.cloned.1.call-update
  7.9 0.0 all-gather.8.cloned.1.call-start
  7.9 0.7 all-gather.8.cloned.1.call-update
  8.6 0.0 all-gather.6.cloned.1.call-start
  9.4 0.7 broadcast_select_fusion.1
  10.0 0.2 convert_reduce_fusion
  10.2 0.7 multiply_add_fusion
  10.9 0.2 compare_reduce_fusion
  11.1 0.1 broadcast_bitcast_fusion
  11.2 67.3 %all-gather.10.cloned.1.call-done = bf16[8,448,192]{1,2,0:T(8,128)(2,1)} async-done(((bf16[1,448,192]{1,2,0:T(8,128)(2,1)}), bf16[8,448,192]{1,2,0:T(8,128)(2,1)}) %all-gather.10.cloned.1.call-update) | async-done | bytes 1376272 | tf_op jit(solution)/shard_map/all_gather | solution.py:41
  78.5 2.3 copy.30
  80.7 1.8 reshape.101
  82.6 63.5 %all-gather.8.cloned.1.call-done = bf16[8,448,192]{1,2,0:T(8,128)(2,1)} async-done(((bf16[1,448,192]{1,2,0:T(8,128)(2,1)}), bf16[8,448,192]{1,2,0:T(8,128)(2,1)}) %all-gather.8.cloned.1.call-update) | async-done | bytes 1376272 | tf_op jit(solution)/shard_map/all_gather | solution.py:42
  146.1 2.3 copy.29
  148.3 2.7 reshape.99
  151.0 0.0 copy-start
  151.0 2.9 fusion.7
  154.0 0.0 copy-done
  154.0 2.8 fusion.12
  156.8 3.6 multiply_convert_fusion
  160.4 0.0 copy-start.1
  160.4 0.6 copy-done.1
  161.1 1.0 stack_reshape.9
  162.1 0.5 maximum_bitcast_fusion.1
  162.5 0.5 copy.31
  163.0 1.2 reshape.96
  164.2 0.0 all-gather.6.cloned.1.call-update
  164.2 0.0 copy-start.2
  164.2 0.0 reduce-scatter.7.cloned.1.call-start
  164.3 2.7 fusion.5
  166.9 0.0 copy-done.2
  167.0 4.2 convolution_add_fusion
  171.1 4.8 copy.37
  175.9 0.0 reduce-scatter.7.cloned.1.call-update
  175.9 0.2 reduce-scatter.9.cloned.1.call-start
  176.2 0.1 dynamic_slice.3
  176.3 83.2 %all-gather.6.cloned.1.call-done = bf16[24,192,384]{2,1,0:T(8,128)(2,1)} async-done(((bf16[3,192,384]{2,1,0:T(8,128)(2,1)}), bf16[24,192,384]{2,1,0:T(8,128)(2,1)}) %all-gather.6.cloned.1.call-update) | async-done | bytes 3538960 | tf_op jit(solution)/shard_map/all_gather | solution.py:74
  259.4 4.6 fusion.19
  264.1 0.1 reshape.97
  264.2 0.4 fusion.42
  264.6 0.2 copy.36
  264.7 0.2 copy.35
  264.9 0.2 copy.34
  265.1 0.7 fusion.2
  265.7 0.7 fusion.1
  266.4 0.7 fusion
  267.1 0.7 maximum_bitcast_fusion
  267.8 2.8 copy.41
  270.6 0.0 copy-start.3
  270.6 0.0 copy-start.4
  270.6 0.0 copy-start.5
  270.6 0.0 reduce-scatter.9.cloned.1.call-update
  270.6 106.2 %reduce-scatter.7.cloned.1.call-done = f32[448,192]{1,0:T(8,128)} async-done(((f32[3584,192]{1,0:T(8,128)}), f32[448,192]{1,0:T(8,128)}) %reduce-scatter.7.cloned.1.call-update) | async-done | bytes 344080
  376.8 1.8 copy.38
  378.6 145.8 %reduce-scatter.9.cloned.1.call-done = bf16[8,10752]{1,0:T(8,128)(2,1)} async-done(((bf16[256,10752]{1,0:T(8,128)(2,1)}), bf16[8,10752]{1,0:T(8,128)(2,1)}) %reduce-scatter.9.cloned.1.call-update) | async-done | bytes 172048
  524.4 0.0 copy-done.3
  524.4 0.0 copy-done.4
  524.5 0.0 copy-done.5
  524.5 2.0 multiply_subtract_fusion
  (6 shorter events, 0.2 us)
Async XLA Ops:
  7.2 71.3 %all-gather.10.cloned.1.call-start = ((), (), s32[]{:S(2)}) async-start(), calls=%async_computation.4 | async-start | bytes 1769472 | tf_op jit(solution)/shard_map/all_gather | solution.py:41
  7.9 138.2 %all-gather.8.cloned.1.call-start = ((), (), s32[]{:S(2)}) async-start(), calls=%async_computation.3 | async-start | bytes 1769472 | tf_op jit(solution)/shard_map/all_gather | solution.py:42
  8.6 250.8 %all-gather.6.cloned.1.call-start = ((), (), s32[]{:S(2)}) async-start(), calls=%async_computation.2 | async-start | bytes 3981312 | tf_op jit(solution)/shard_map/all_gather | solution.py:74
  151.0 2.9 copy-start
  160.4 0.7 copy-start.1
  164.2 2.7 copy-start.2
  164.2 212.6 %reduce-scatter.7.cloned.1.call-start = ((), (), s32[]{:S(2)}) async-start(), calls=%async_computation.5 | async-start | bytes 4128768
  175.9 348.5 %reduce-scatter.9.cloned.1.call-start = ((), (), s32[]{:S(2)}) async-start(), calls=%async_computation.6 | async-start | bytes 5677056
  270.6 253.9 %copy-start.3 = (f32[3,8,3584]{2,1,0:T(8,128)S(1)}, f32[3,8,3584]{2,1,0:T(8,128)}, u32[]{:S(2)}) copy-start(f32[3,8,3584]{2,1,0:T(8,128)} %param.13) | copy-start | bytes 1032196
  270.6 253.9 %copy-start.4 = (f32[3,8,3584]{2,1,0:T(8,128)S(1)}, f32[3,8,3584]{2,1,0:T(8,128)}, u32[]{:S(2)}) copy-start(f32[3,8,3584]{2,1,0:T(8,128)} %param.14) | copy-start | bytes 1032196
  270.6 253.9 %copy-start.5 = (f32[3,8,3584]{2,1,0:T(8,128)S(1)}, f32[3,8,3584]{2,1,0:T(8,128)}, u32[]{:S(2)}) copy-start(f32[3,8,3584]{2,1,0:T(8,128)} %param.15) | copy-start | bytes 1032196
Sparse Core Ops, SparseCore 0:
  10.6 67.8 all-gather.9
  81.1 64.9 all-gather.7
  164.3 95.0 all-gather.5
  263.5 113.2 reduce-scatter.6
  379.4 145.0 reduce-scatter.8
where the time goes:
time: 539 us; the launch traced here: 533 us
  waiting for transfers between devices  467 us (87%)
  local copies, waits for them, and re-layouts  22.8 us (4%)
  matrix products  22.8 us (4%)
  between operations  14.6 us (3%)
    unnamed x7, waiting for transfers between devices  253 us
    all_gather x1, waiting for transfers between devices, per_device(): shard_piece = lax.all_gather(packed, 'tp', axis=0, tiled=True)  83.2 us
    all_gather x1, waiting for transfers between devices, per_device(): lax.all_gather(tokens, 'tp', axis=1, tiled=True)  67.3 us
    all_gather x1, waiting for transfers between devices, per_device(): lax.all_gather(cotangent, 'tp', axis=1, tiled=True)  63.5 us
    unnamed x17, local copies, waits for them, and re-layouts  14.5 us
  transfers between devices with their start and end apart: 5, of which 5 were waited for; matrix products, arithmetic and copies ran while one was open for 6% of the time, Pallas kernels for 0%

commit v1 on v0

v1 whole, which is shorter than its diff:
```python
import jax
import jax.numpy as jnp
from jax import lax
from jax.experimental import pallas as pl
from jax.experimental.pallas import tpu as pltpu
from jax.sharding import PartitionSpec as P

MESH = pl.DeviceIdType.MESH
F32, BF16 = jnp.float32, jnp.bfloat16

D = 3584
BLOCK = 128
BLOCKS = 16
SLOTS = 3
TOK = 192
N_Y, N_ZH, N_X, N_ZL = 4, 2, 4, 4
N_TP = N_Y * N_ZH
REPLICAS = N_X * N_ZL * 2
SHARD = D // N_TP
HALF = D // 2
COLS = 256
CHUNKS = HALF // COLS
ROWS = 16

beta_one = 0.9
beta_two = 0.95
learn_rate = 0.05
decay_rate = 0.1
adam_eps = 1e-08
bias_one = 1.0 - 0.9**10
bias_two = 1.0 - 0.95**10

NT = (((1,), (1,)), ((), ()))


def kernel(
    tok, cot, work, flag, bmap, master, mom_one, mom_two,
    ig_out, master_out, one_out, two_out,
    w, state, land, xfull, gfull, xo, go,
    mask, fill, acts, contrib, act_land, act_zsend, act_zland, fin, fin_o, lhs, lhs_o,
    ig_send, ig_land, ig_zsend, ig_zland, ig_own,
    g_send, x_land, x_sum, z_send, z_land, c_own, c_land,
    w_sem, state_sem, p1_s, p1_r, cx_s, cx_r,
    act_s, act_r, az_s, az_r, ac_s, ac_r,
    ig_s, ig_r, iz_s, iz_r,
    x_s, x_r, z_s, z_r, c_s, c_r,
):
    dp, tp = lax.axis_index("dp"), lax.axis_index("tp")
    zl, x, c = lax.div(dp, 8), lax.rem(lax.div(dp, 2), 4), lax.rem(dp, 2)
    zh, y = lax.div(tp, 4), lax.rem(tp, 4)
    oh = 1 - zh

    def at(zh_, y_):
        return zh_ * 4 + y_

    def y_dev(j):
        return (dp, at(zh, lax.rem(y + j, 4)))

    def x_dev(j):
        return (zl * 8 + lax.rem(x + j, 4) * 2 + c, tp)

    def z_dev(j):
        return (lax.rem(zl + j, 4) * 8 + x * 2 + c, tp)

    anti = at(oh, y)
    anti_dev = (dp, anti)
    core_dev = (zl * 8 + x * 2 + (1 - c), tp)

    def remote(src, dst, ssem, rsem, dev):
        return pltpu.make_async_remote_copy(
            src_ref=src, dst_ref=dst, send_sem=ssem, recv_sem=rsem, device_id=dev, device_id_type=MESH
        )

    barrier = pltpu.get_barrier_semaphore()
    for dev in [y_dev(1), y_dev(2), y_dev(3), anti_dev, core_dev, x_dev(1), x_dev(2), x_dev(3), z_dev(1), z_dev(2), z_dev(3)]:
        pl.semaphore_signal(barrier, inc=1, device_id=dev, device_id_type=MESH)

    w_copies = [pltpu.make_async_copy(work.at[k], w.at[k], w_sem.at[k]) for k in range(3)]
    for cp in w_copies:
        cp.start()
    state_copies = [
        pltpu.make_async_copy(ref, state.at[i], state_sem.at[i]) for i, ref in enumerate((master, mom_one, mom_two))
    ]
    for cp in state_copies:
        cp.start()
    land[tp, 0] = tok[...]
    land[tp, 1] = cot[...]

    count = jnp.int32(0)
    filled = [jnp.float32(0.0)] * SLOTS
    for b in range(BLOCKS):
        holder = jnp.where(flag[0] > 0, bmap[0, b], b // 2)
        mine = jnp.where(holder == tp, 1, 0)
        for s in range(SLOTS):
            hit = (mine * jnp.where(count == s, 1, 0)).astype(F32)
            mask[b * SLOTS + s] = hit
            filled[s] = filled[s] + hit
        count = count + mine
    for s in range(SLOTS):
        fill[s] = filled[s]

    pl.semaphore_wait(barrier, 11)

    right, left = y_dev(1), y_dev(3)
    yr, yl = lax.rem(y + 1, 4), lax.rem(y + 3, 4)
    p1 = {}

    def send(index, chunk, a, dev):
        cp = remote(land.at[chunk, a], land.at[chunk, a], p1_s.at[index], p1_r.at[index], dev)
        cp.start()
        p1[index] = cp

    send(0, tp, 0, anti_dev)
    send(2, tp, 0, right)
    send(5, tp, 1, left)
    send(1, tp, 1, anti_dev)
    send(3, tp, 1, right)
    send(4, tp, 0, left)
    p1[2].wait_recv()
    send(6, at(zh, yl), 0, right)
    p1[5].wait_recv()
    send(7, at(zh, yr), 1, left)
    p1[0].wait_recv()
    send(8, anti, 0, right)
    send(10, anti, 0, left)
    p1[1].wait_recv()
    send(11, anti, 1, left)
    send(9, anti, 1, right)
    p1[8].wait_recv()
    send(12, at(oh, yl), 0, right)
    p1[11].wait_recv()
    send(13, at(oh, yr), 1, left)
    for index in (3, 4, 6, 7, 9, 10, 12, 13):
        p1[index].wait_recv()

    for j in range(N_TP):
        xfull[:, j * SHARD : (j + 1) * SHARD] = land[j, 0]
        gfull[:, j * SHARD : (j + 1) * SHARD] = land[j, 1]

    other_cols = pl.ds(pl.multiple_of((1 - c) * HALF, HALF), HALF)
    cx = [
        remote(xfull.at[:, other_cols], xo, cx_s.at[0], cx_r.at[0], core_dev),
        remote(gfull.at[:, other_cols], go, cx_s.at[1], cx_r.at[1], core_dev),
    ]
    for cp in cx:
        cp.start()

    for cp in w_copies:
        cp.wait()
    zg = lax.dot_general(xfull[...], w[0], NT, preferred_element_type=F32)
    zu = lax.dot_general(xfull[...], w[1], NT, preferred_element_type=F32)
    dh = lax.dot_general(gfull[...], w[2], NT, preferred_element_type=F32)
    sig = jax.nn.sigmoid(zg)
    active = zg * sig
    kinds = (
        (dh * zu * sig * (1.0 + zg * (1.0 - sig))).astype(BF16),
        (dh * active).astype(BF16),
        (active * zu).astype(BF16),
    )
    for k in range(3):
        for s in range(SLOTS):
            acts[s, k] = kinds[k][:, s * BLOCK : (s + 1) * BLOCK]

    def contribute(owner):
        for i in range(2):
            base = (owner * 2 + i) * SLOTS
            m = [jnp.full((TOK, BLOCK), mask[base + s], F32).astype(BF16) for s in range(SLOTS)]
            for k in range(3):
                contrib[owner, i * 3 + k] = acts[0, k] * m[0] + acts[1, k] * m[1] + acts[2, k] * m[2]

    act = {}
    for part, zt in ((0, oh), (1, zh)):
        for j in (2, 1, 3):
            owner = at(zt, lax.rem(y + j, 4))
            contribute(owner)
            cp = remote(
                contrib.at[owner], act_land.at[j - 1, part], act_s.at[j - 1, part], act_r.at[j - 1, part], y_dev(j)
            )
            cp.start()
            act[j, part] = cp
    contribute(anti)
    contribute(tp)

    gate_m = jnp.concatenate(
        [acts[s, 0] * jnp.full((TOK, BLOCK), fill[s], F32).astype(BF16) for s in range(SLOTS)], axis=1
    )
    up_m = jnp.concatenate(
        [acts[s, 1] * jnp.full((TOK, BLOCK), fill[s], F32).astype(BF16) for s in range(SLOTS)], axis=1
    )
    for p in range(N_TP // 2):
        cols = slice(p * 2 * SHARD, (p + 1) * 2 * SHARD)
        value = (
            jnp.dot(gate_m, w[0, :, cols], preferred_element_type=F32)
            + jnp.dot(up_m, w[1, :, cols], preferred_element_type=F32)
        ).astype(BF16)
        ig_send[2 * p] = value[:, :SHARD]
        ig_send[2 * p + 1] = value[:, SHARD:]

    for j in (2, 1, 3):
        act[j, 0].wait_recv()
    for i in range(6):
        act_zsend[i] = (contrib[anti, i] + act_land[0, 0, i]) + (act_land[1, 0, i] + act_land[2, 0, i])
    az = remote(act_zsend, act_zland, az_s, az_r, anti_dev)
    az.start()
    for j in (2, 1, 3):
        act[j, 1].wait_recv()

    ig = {}
    for part, zt in ((0, oh), (1, zh)):
        for j in (2, 1, 3):
            owner = at(zt, lax.rem(y + j, 4))
            cp = remote(
                ig_send.at[owner], ig_land.at[j - 1, part], ig_s.at[j - 1, part], ig_r.at[j - 1, part], y_dev(j)
            )
            cp.start()
            ig[j, part] = cp

    for i in range(6):
        fin[i] = (contrib[tp, i] + act_land[0, 1, i]) + (act_land[1, 1, i] + act_land[2, 1, i])
    az.wait_recv()
    for i in range(6):
        fin[i] = fin[i] + act_zland[i]
    ac = remote(fin, fin_o, ac_s, ac_r, core_dev)
    ac.start()
    for k in range(3):
        for i in range(2):
            lhs[k, i * BLOCK : (i + 1) * BLOCK, :] = fin[i * 3 + k].T
    for cp in cx:
        cp.wait_recv()
    ac.wait_recv()
    for k in range(3):
        for i in range(2):
            lhs_o[k, i * BLOCK : (i + 1) * BLOCK, :] = fin_o[i * 3 + k].T

    def x_copy(n, j):
        return remote(
            g_send.at[n, lax.rem(x + j, 4)], x_land.at[n, j - 1], x_s.at[n, j - 1], x_r.at[n, j - 1], x_dev(j)
        )

    def z_copy(n, j):
        return remote(
            z_send.at[n, lax.rem(zl + j, 4)], z_land.at[n, j - 1], z_s.at[n, j - 1], z_r.at[n, j - 1], z_dev(j)
        )

    @pl.loop(0, CHUNKS)
    def _(n):
        mine = pl.ds(pl.multiple_of(c * HALF + n * COLS, COLS), COLS)
        cols = pl.ds(pl.multiple_of(n * COLS, COLS), COLS)
        for k in range(3):
            own, other = (xfull, xo) if k < 2 else (gfull, go)
            value = (
                jnp.dot(lhs[k], own[:, mine], preferred_element_type=F32)
                + jnp.dot(lhs_o[k], other[:, cols], preferred_element_type=F32)
            ).astype(BF16)
            for zt in range(N_ZL):
                for xt in range(N_X):
                    row = (zt * N_X + xt) * ROWS
                    g_send[n, xt, zt, k] = value[row : row + ROWS]
        for j in (2, 1, 3):
            x_copy(n, j).start()

    for j in (2, 1, 3):
        ig[j, 0].wait_recv()
    ig_zsend[...] = (
        (ig_send[anti].astype(F32) + ig_land[0, 0].astype(F32))
        + (ig_land[1, 0].astype(F32) + ig_land[2, 0].astype(F32))
    ).astype(BF16)
    iz = remote(ig_zsend, ig_zland, iz_s, iz_r, anti_dev)
    iz.start()
    for j in (2, 1, 3):
        ig[j, 1].wait_recv()
    ig_own[...] = (ig_send[tp].astype(F32) + ig_land[0, 1].astype(F32)) + (
        ig_land[1, 1].astype(F32) + ig_land[2, 1].astype(F32)
    )

    @pl.loop(0, CHUNKS)
    def _(n):
        for j in (1, 3, 2):
            x_copy(n, j).wait_recv()
        for zt in range(N_ZL):
            for k in range(3):
                value = (g_send[n, x, zt, k].astype(F32) + x_land[n, 0, zt, k].astype(F32)) + (
                    x_land[n, 1, zt, k].astype(F32) + x_land[n, 2, zt, k].astype(F32)
                )
                x_sum[n, zt, k] = value
                z_send[n, zt, k] = value.astype(BF16)
        for j in (3, 2, 1):
            z_copy(n, j).start()

    iz.wait_recv()
    ig_out[...] = (ig_own[...] + ig_zland[...].astype(F32)).astype(BF16)

    @pl.loop(0, CHUNKS)
    def _(n):
        cols = pl.ds(pl.multiple_of(n * COLS, COLS), COLS)
        for j in (1, 2, 3):
            z_copy(n, j).wait_recv()
        for k in range(3):
            value = (x_sum[n, zl, k] + z_land[n, 0, k].astype(F32)) + (
                z_land[n, 1, k].astype(F32) + z_land[n, 2, k].astype(F32)
            )
            c_own[0, k, :, cols] = value[:8]
            c_own[1, k, :, cols] = value[8:]

    cc = remote(c_own.at[1 - c], c_land, c_s, c_r, core_dev)
    cc.start()
    for cp in state_copies:
        cp.wait()

    def adam(read, start):
        cols = pl.ds(pl.multiple_of(start, HALF), HALF)
        for k in range(3):
            grad = read(k) * (1.0 / REPLICAS)
            one = beta_one * state[1, k, :, cols] + (1.0 - beta_one) * grad
            two = beta_two * state[2, k, :, cols] + (1.0 - beta_two) * grad * grad
            old = state[0, k, :, cols]
            update = one / bias_one / (jnp.sqrt(two / bias_two) + adam_eps) + decay_rate * old
            master_out[k, :, cols] = old - learn_rate * update
            one_out[k, :, cols] = one
            two_out[k, :, cols] = two

    adam(lambda k: c_own[c, k], c * HALF)
    cc.wait_recv()
    adam(lambda k: c_land[k], (1 - c) * HALF)

    for cp in p1.values():
        cp.wait_send()
    for cp in cx + list(act.values()) + [az, ac] + list(ig.values()) + [iz, cc]:
        cp.wait_send()

    @pl.loop(0, CHUNKS)
    def _(n):
        for j in (1, 2, 3):
            x_copy(n, j).wait_send()
            z_copy(n, j).wait_send()


def per_device(tokens, cotangent, working, degraded, block_map, master, moment_one, moment_two):
    vmem = pl.BlockSpec(memory_space=pltpu.VMEM)
    smem = pl.BlockSpec(memory_space=pltpu.SMEM)
    hbm = pl.BlockSpec(memory_space=pl.ANY)
    dma = pltpu.SemaphoreType.DMA
    rows = (3, 8, D)
    return pl.pallas_call(
        kernel,
        name="swiglu_step",
        out_shape=(
            jax.ShapeDtypeStruct((TOK, SHARD), BF16),
            jax.ShapeDtypeStruct(rows, F32),
            jax.ShapeDtypeStruct(rows, F32),
            jax.ShapeDtypeStruct(rows, F32),
        ),
        in_specs=[vmem, vmem, hbm, smem, smem, hbm, hbm, hbm],
        out_specs=(vmem,) * 4,
        scratch_shapes=[
            pltpu.VMEM((3, SLOTS * BLOCK, D), BF16),
            pltpu.VMEM((3,) + rows, F32),
            pltpu.VMEM((N_TP, 2, TOK, SHARD), BF16),
            pltpu.VMEM((TOK, D), BF16),
            pltpu.VMEM((TOK, D), BF16),
            pltpu.VMEM((TOK, HALF), BF16),
            pltpu.VMEM((TOK, HALF), BF16),
            pltpu.SMEM((BLOCKS * SLOTS,), F32),
            pltpu.SMEM((SLOTS,), F32),
            pltpu.VMEM((SLOTS, 3, TOK, BLOCK), BF16),
            pltpu.VMEM((N_TP, 6, TOK, BLOCK), BF16),
            pltpu.VMEM((3, 2, 6, TOK, BLOCK), BF16),
            pltpu.VMEM((6, TOK, BLOCK), BF16),
            pltpu.VMEM((6, TOK, BLOCK), BF16),
            pltpu.VMEM((6, TOK, BLOCK), BF16),
            pltpu.VMEM((6, TOK, BLOCK), BF16),
            pltpu.VMEM((3, 2 * BLOCK, TOK), BF16),
            pltpu.VMEM((3, 2 * BLOCK, TOK), BF16),
            pltpu.VMEM((N_TP, TOK, SHARD), BF16),
            pltpu.VMEM((3, 2, TOK, SHARD), BF16),
            pltpu.VMEM((TOK, SHARD), BF16),
            pltpu.VMEM((TOK, SHARD), BF16),
            pltpu.VMEM((TOK, SHARD), F32),
            pltpu.VMEM((CHUNKS, N_X, N_ZL, 3, ROWS, COLS), BF16),
            pltpu.VMEM((CHUNKS, 3, N_ZL, 3, ROWS, COLS), BF16),
            pltpu.VMEM((CHUNKS, N_ZL, 3, ROWS, COLS), F32),
            pltpu.VMEM((CHUNKS, N_ZL, 3, ROWS, COLS), BF16),
            pltpu.VMEM((CHUNKS, 3, 3, ROWS, COLS), BF16),
            pltpu.VMEM((2, 3, 8, HALF), F32),
            pltpu.VMEM((3, 8, HALF), F32),
            dma((3,)),
            dma((3,)),
            dma((14,)),
            dma((14,)),
            dma((2,)),
            dma((2,)),
            dma((3, 2)),
            dma((3, 2)),
            dma,
            dma,
            dma,
            dma,
            dma((3, 2)),
            dma((3, 2)),
            dma,
            dma,
            dma((CHUNKS, 3)),
            dma((CHUNKS, 3)),
            dma((CHUNKS, 3)),
            dma((CHUNKS, 3)),
            dma,
            dma,
        ],
        compiler_params=pltpu.CompilerParams(
            collective_id=0, has_side_effects=True, vmem_limit_bytes=60 * 1024 * 1024
        ),
        cost_estimate=pl.CostEstimate(flops=3_700_000_000, bytes_accessed=12_000_000, transcendentals=73728),
    )(tokens, cotangent, working.reshape(working.shape[2:]), degraded, block_map, master, moment_one, moment_two)


def solution(mesh):
    return jax.shard_map(
        per_device,
        mesh=mesh,
        in_specs=(
            P("dp", "tp"),
            P("dp", "tp"),
            P("dp", "tp", None, None, None),
            P("dp"),
            P("dp", None),
            P(None, ("tp", "dp"), None),
            P(None, ("tp", "dp"), None),
            P(None, ("tp", "dp"), None),
        ),
        out_specs=(
            P("dp", "tp"),
            P(None, ("tp", "dp"), None),
            P(None, ("tp", "dp"), None),
            P(None, ("tp", "dp"), None),
        ),
        check_vma=False,
    )
```

time: 539 us -> 128 us (0.24); the launches traced: 533 us -> 128 us
  waiting for transfers between devices: 467 us -> 0 us
  Pallas kernels: 0 us -> 119 us
  matrix products: 22.8 us -> 0 us
  local copies, waits for them, and re-layouts: 22.8 us -> 6.81 us
  between operations: 14.6 us -> 1.29 us
    unnamed x7 -> x0, waiting for transfers between devices: 253 us -> none
    all_gather x3 -> x0, waiting for transfers between devices: 214 us -> none  [the longest x1 83.2 us: per_device(): shard_piece = lax.all_gather(packed, 'tp', axis=0, tiled=True)]
    pallas_call x0 -> x1, Pallas kernels: none -> 119 us  [per_device(): pl.pallas_call(kernel, name='swiglu_step', out_shape=(jax.ShapeDtypeStruc...]
    dot_general x9 -> x0, matrix products: 22.8 us -> none  [the longest x1 4.59 us: per_device(): jnp.einsum('kn,ntc->ktc', selector, shard_piece, preferred_element_type=j...]
    unnamed x17 -> x4, local copies, waits for them, and re-layouts: 14.5 us -> 6.81 us
  transfers between devices with their start and end apart: 5 -> 0, of which waited for: 5 -> 0; matrix products, arithmetic and copies ran while one was open for 6% -> 0% of each run, Pallas kernels for 0% -> 0%
where the time goes in v1:
time: 128 us
  Pallas kernels  119 us (93%)
  local copies, waits for them, and re-layouts  6.81 us (5%)
  between operations  1.29 us (1%)
    pallas_call x1, Pallas kernels, per_device(): pl.pallas_call(kernel, name='swiglu_step', out_shape=(jax.ShapeDtypeStruc...  119 us
    unnamed x4, local copies, waits for them, and re-layouts  6.81 us

profile of v1, /device:TPU:25, one launch (start us, length us, event | category | flops | bytes accessed | tf_op | source)
XLA Modules:
  0.0 127.6 jit_solution(3660488797436360415)
XLA Ops:
  1.3 119.5 %swiglu_step.1 = (bf16[192,448]{1,0:T(8,128)(2,1)}, f32[3,8,3584]{2,1,0:T(8,128)}, f32[3,8,3584]{2,1,0:T(8,128)}, f32[3,8,3584]{2,1,0:T(8,128)}) custom-call(bf16[192,448]{1,0:T(8,128)(2,1)} %tok.1, bf16[192,448]{1,0:T(8,128)(2,1)} %cot.1, bf16[3,384,3584]{2,1,0:T(8,128)(2,1)} %bitcast.1, s32[1]{0:T(128)S(6)} %copy.16.flag, s32[1,16]{1,0:T(1,128)} %bmap.1, ...), custom_call_target="tpu_custom_call" | custom-call | flops 3700000000 | bytes 12000000 | tf_op jit(solution)/shard_map/swiglu_step/pallas_call | solution.py:344
  120.8 1.6 %copy.17 = bf16[192,448]{1,0:T(8,128)(2,1)} copy(bf16[192,448]{1,0:T(8,128)(2,1)} %get-tuple-element.8) | data formatting | bytes 344064
  122.4 1.7 %copy.18 = f32[3,8,3584]{2,1,0:T(8,128)} copy(f32[3,8,3584]{2,1,0:T(8,128)} %get-tuple-element.9) | data formatting | bytes 688128
  124.1 1.7 %copy.19 = f32[3,8,3584]{2,1,0:T(8,128)} copy(f32[3,8,3584]{2,1,0:T(8,128)} %get-tuple-element.10) | data formatting | bytes 688128
  125.8 1.7 %copy.20 = f32[3,8,3584]{2,1,0:T(8,128)} copy(f32[3,8,3584]{2,1,0:T(8,128)} %get-tuple-element.11) | data formatting | bytes 688128

commit v2 on v0

v2 whole, which is shorter than its diff:
```python
import jax
import jax.numpy as jnp
from jax import lax
from jax.experimental import pallas as pl
from jax.experimental.pallas import tpu as pltpu
from jax.sharding import PartitionSpec as P

MESH = pl.DeviceIdType.MESH
F32, BF16 = jnp.float32, jnp.bfloat16

D = 3584
BLOCK = 128
BLOCKS = 16
SLOTS = 3
TOK = 192
N_Y, N_ZH, N_X, N_ZL = 4, 2, 4, 4
N_TP = N_Y * N_ZH
REPLICAS = N_X * N_ZL * 2
SHARD = D // N_TP
GROUP = 2 * N_X
UNIT = SLOTS * TOK
EARLY, LATE = (0, TOK // 2), (TOK // 2, TOK // 2)

beta_one = 0.9
beta_two = 0.95
learn_rate = 0.05
decay_rate = 0.1
adam_eps = 1e-08
bias_one = 1.0 - 0.9**10
bias_two = 1.0 - 0.95**10

NT = (((1,), (1,)), ((), ()))


def kernel(
    tok, cot, work, flag, bmap,
    ig_out, grad_out,
    w, land, xl, xfull, gfull,
    place, fill, ab, own_sel, az_send, az_land, ftb,
    ig_send, ig_land, ig_zsend, ig_zland, ig_own, act_f,
    part, z_send, z_land, tr, gl,
    w_sem, p1_s, p1_r, xs_s, xs_r,
    ya_s, ya_r, az_s, az_r, xa_s, xa_r,
    ig_s, ig_r, iz_s, iz_r,
    z_s, z_r, tr_s, tr_r,
):
    dp, tp = lax.axis_index("dp"), lax.axis_index("tp")
    zl, x, c = lax.div(dp, 8), lax.rem(lax.div(dp, 2), 4), lax.rem(dp, 2)
    zh, y = lax.div(tp, 4), lax.rem(tp, 4)
    oh = 1 - zh
    oc = 1 - c
    me = c * 4 + x
    seat = x * 2 + c

    def at(zh_, y_):
        return zh_ * 4 + y_

    def y_dev(j):
        return (dp, at(zh, lax.rem(y + j, 4)))

    def group_dev(x_, c_):
        return (zl * 8 + x_ * 2 + c_, tp)

    def z_dev(j):
        return (lax.rem(zl + j, 4) * 8 + x * 2 + c, tp)

    def x_at(j):
        return lax.rem(x + j, 4)

    anti = at(oh, y)
    anti_dev = (dp, anti)
    core_dev = group_dev(x, oc)

    def remote(src, dst, ssem, rsem, dev):
        return pltpu.make_async_remote_copy(
            src_ref=src, dst_ref=dst, send_sem=ssem, recv_sem=rsem, device_id=dev, device_id_type=MESH
        )

    sent = []

    def start(src, dst, ssem, rsem, dev):
        cp = remote(src, dst, ssem, rsem, dev)
        cp.start()
        sent.append(cp)
        return cp

    barrier = pltpu.get_barrier_semaphore()
    partners = [y_dev(1), y_dev(2), y_dev(3), anti_dev, core_dev]
    partners += [group_dev(x_at(j), t) for j in (1, 2, 3) for t in (c, oc)]
    partners += [z_dev(1), z_dev(2), z_dev(3)]
    for dev in partners:
        pl.semaphore_signal(barrier, inc=1, device_id=dev, device_id_type=MESH)

    own_copies = [pltpu.make_async_copy(ref, land.at[tp, a], w_sem.at[3 + a]) for a, ref in ((0, tok), (1, cot))]
    for cp in own_copies:
        cp.start()
    w_copies = [pltpu.make_async_copy(work.at[k], w.at[k], w_sem.at[k]) for k in range(3)]
    for cp in w_copies:
        cp.start()

    holders = [jnp.where(flag[0] > 0, bmap[0, b], b // 2) for b in range(BLOCKS)]
    filled = [jnp.float32(0.0)] * SLOTS
    for b in range(BLOCKS):
        rank = jnp.int32(0)
        for e in range(b):
            rank = rank + jnp.where(holders[e] == holders[b], 1, 0)
        spot = holders[b] * SLOTS + rank
        place[b] = spot
        for s in range(SLOTS):
            filled[s] = filled[s] + jnp.where(spot == tp * SLOTS + s, 1.0, 0.0)
    for s in range(SLOTS):
        fill[s] = filled[s]

    for cp in own_copies:
        cp.wait()
    pl.semaphore_wait(barrier, len(partners))

    right, left = y_dev(1), y_dev(3)
    yr, yl = lax.rem(y + 1, 4), lax.rem(y + 3, 4)
    p1 = {}

    def send(a, index, chunk, dev, rows=(0, TOK)):
        ref = land.at[chunk, a, pl.ds(*rows)]
        p1[a, index] = start(ref, ref, p1_s.at[a, index], p1_r.at[a, index], dev)

    def neighbours(a, half):
        chunk = (tp, anti)[half]
        send(a, 1 + 4 * half, chunk, right)
        send(a, 2 + 4 * half, chunk, left)

    def forward(a, half):
        zt = (zh, oh)[half]
        p1[a, 1 + 4 * half].wait_recv()
        send(a, 3 + 4 * half, at(zt, yl), right, EARLY)
        p1[a, 2 + 4 * half].wait_recv()
        send(a, 4 + 4 * half, at(zt, yr), left, LATE)

    def slices(a, half):
        p1[a, 3 + 4 * half].wait_recv()
        p1[a, 4 + 4 * half].wait_recv()
        zt = (zh, oh)[half]
        for j in (2, 1, 3):
            start(
                land.at[at(zt, x_at(j)), a],
                xl.at[me, a],
                xs_s.at[half * 3 + j - 1, a],
                xs_r.at[me, a],
                group_dev(x_at(j), zt),
            )

    def core_slice(a):
        start(land.at[oc * 4 + x, a], xl.at[me, a], xs_s.at[6, a], xs_r.at[me, a], core_dev)

    send(0, 0, tp, anti_dev)
    neighbours(0, 0)
    send(1, 0, tp, anti_dev)
    forward(0, 0)
    neighbours(1, 0)
    p1[0, 0].wait_recv()
    neighbours(0, 1)
    forward(1, 0)
    slices(0, 0)
    forward(0, 1)
    p1[1, 0].wait_recv()
    neighbours(1, 1)
    slices(1, 0)
    slices(0, 1)
    core_slice(0)

    ya = {}

    def y_send(k, value):
        value = value.astype(BF16)
        for s in range(SLOTS):
            ab[y, k, s * TOK : (s + 1) * TOK] = value[:, s * BLOCK : (s + 1) * BLOCK]
        for q, dev in ((0, right), (1, left)):
            ya[k, q] = start(ab.at[y, k], ab.at[y, k], ya_s.at[k, q], ya_r.at[k, q], dev)

    lower, upper = pl.ds(0, UNIT // 2), pl.ds(UNIT // 2, UNIT // 2)

    def y_forward(k):
        ya[k, 0].wait_recv()
        ya[k, 2] = start(ab.at[yl, k, lower], ab.at[yl, k, lower], ya_s.at[k, 2], ya_r.at[k, 2], right)
        ya[k, 1].wait_recv()
        ya[k, 3] = start(ab.at[yr, k, upper], ab.at[yr, k, upper], ya_s.at[k, 3], ya_r.at[k, 3], left)

    for j in range(N_TP):
        xfull[:, j * SHARD : (j + 1) * SHARD] = land[j, 0]
    w_copies[0].wait()
    w_copies[1].wait()
    zg = lax.dot_general(xfull[...], w[0], NT, preferred_element_type=F32)
    zu = lax.dot_general(xfull[...], w[1], NT, preferred_element_type=F32)
    sig = jax.nn.sigmoid(zg)
    active = zg * sig
    y_send(2, active * zu)
    act_f[0] = active
    act_f[1] = zu * sig * (1.0 + zg * (1.0 - sig))

    forward(1, 1)
    y_forward(2)
    slices(1, 1)
    core_slice(1)
    for j in range(N_TP):
        gfull[:, j * SHARD : (j + 1) * SHARD] = land[j, 1]
    w_copies[2].wait()
    dh = lax.dot_general(gfull[...], w[2], NT, preferred_element_type=F32)
    y_send(1, dh * act_f[0])
    y_send(0, dh * act_f[1])

    def ig_multiply():
        def masked(k):
            return jnp.concatenate(
                [
                    ab[y, k, s * TOK : (s + 1) * TOK] * jnp.full((TOK, BLOCK), fill[s], F32).astype(BF16)
                    for s in range(SLOTS)
                ],
                axis=1,
            )

        gate_m, up_m = masked(0), masked(1)
        for p in range(N_TP // 2):
            cols = slice(p * 2 * SHARD, (p + 1) * 2 * SHARD)
            value = (
                jnp.dot(gate_m, w[0, :, cols], preferred_element_type=F32)
                + jnp.dot(up_m, w[1, :, cols], preferred_element_type=F32)
            ).astype(BF16)
            ig_send[2 * p] = value[:, :SHARD]
            ig_send[2 * p + 1] = value[:, SHARD:]

    def select(k, owner, i):
        spot = place[owner * 2 + i]
        total = None
        for yt in range(N_Y):
            for s in range(SLOTS):
                m = jnp.where(spot == at(zh, yt) * SLOTS + s, 1.0, 0.0)
                term = ab[yt, k, s * TOK : (s + 1) * TOK] * jnp.full((TOK, BLOCK), m, F32).astype(BF16)
                total = term if total is None else total + term
        return total

    az = {}

    def y_select(k):
        ya[k, 2].wait_recv()
        ya[k, 3].wait_recv()
        for i in range(2):
            az_send[k, i] = select(k, anti, i)
        az[k] = start(az_send.at[k], az_land.at[k], az_s.at[k], az_r.at[k], anti_dev)
        for i in range(2):
            own_sel[k, i] = select(k, tp, i)

    x_right, x_left = group_dev(x_at(1), c), group_dev(x_at(3), c)
    top, bottom = pl.ds(0, BLOCK), pl.ds(BLOCK, BLOCK)
    xa = {}

    def x_send(k, q, ref, dev):
        xa[k, q] = start(ref, ref, xa_s.at[k, q], xa_r.at[k, q], dev)

    def x_first(k):
        az[k].wait_recv()
        for i in range(2):
            ftb[me, k, i * BLOCK : (i + 1) * BLOCK, :] = (own_sel[k, i] + az_land[k, i]).T
        x_send(k, 0, ftb.at[me, k], x_right)
        x_send(k, 1, ftb.at[me, k], x_left)
        x_send(k, 4, ftb.at[me, k], core_dev)

    def x_forward(k):
        xa[k, 0].wait_recv()
        x_send(k, 2, ftb.at[c * 4 + x_at(3), k, top], x_right)
        x_send(k, 5, ftb.at[c * 4 + x_at(3), k], core_dev)
        xa[k, 1].wait_recv()
        x_send(k, 3, ftb.at[c * 4 + x_at(1), k, bottom], x_left)
        x_send(k, 6, ftb.at[c * 4 + x_at(1), k], core_dev)

    def x_last(k):
        xa[k, 2].wait_recv()
        xa[k, 3].wait_recv()
        x_send(k, 7, ftb.at[c * 4 + x_at(2), k], core_dev)

    zz = {}

    def z_first(k):
        for q in (4, 5, 6, 7):
            xa[k, q].wait_recv()
        a = 0 if k < 2 else 1
        total = None
        for g in range(GROUP):
            term = jnp.dot(ftb[g, k], xl[g, a], preferred_element_type=F32)
            total = term if total is None else total + term
        for zt in range(N_ZL):
            piece = total[zt * 64 : (zt + 1) * 64]
            part[k, zt] = piece
            z_send[k, zt] = piece.astype(BF16)
        for j in (2, 1, 3):
            zz[k, j] = start(
                z_send.at[k, lax.rem(zl + j, 4)], z_land.at[k, j - 1], z_s.at[k, j - 1], z_r.at[k, j - 1], z_dev(j)
            )

    rows = {}

    def rows_first(k):
        for j in (1, 2, 3):
            zz[k, j].wait_recv()
        value = (part[k, zl] + z_land[k, 0].astype(F32)) + (z_land[k, 1].astype(F32) + z_land[k, 2].astype(F32))
        tr[k] = (value * (1.0 / REPLICAS)).reshape(GROUP, 8, SHARD)
        for r in range(1, GROUP):
            q = lax.rem(seat + r, GROUP)
            rows[k, r] = start(
                tr.at[k, q], gl.at[k, me], tr_s.at[k, r - 1], tr_r.at[k, r - 1], group_dev(lax.div(q, 2), lax.rem(q, 2))
            )
        gl[k, me] = tr[k, seat]

    def rows_last(k):
        for r in range(1, GROUP):
            rows[k, r].wait_recv()
        for g in range(GROUP):
            grad_out[k, :, g * SHARD : (g + 1) * SHARD] = gl[k, g]

    ig = {}

    def ig_first():
        for half, zt in ((0, oh), (1, zh)):
            for j in (2, 1, 3):
                ig[half, j] = start(
                    ig_send.at[at(zt, lax.rem(y + j, 4))],
                    ig_land.at[j - 1, half],
                    ig_s.at[j - 1, half],
                    ig_r.at[j - 1, half],
                    y_dev(j),
                )

    def ig_sum(half, owner):
        for j in (1, 2, 3):
            ig[half, j].wait_recv()
        return (ig_send[owner].astype(F32) + ig_land[0, half].astype(F32)) + (
            ig_land[1, half].astype(F32) + ig_land[2, half].astype(F32)
        )

    def slices_wait():
        for r in range(1, GROUP):
            g = lax.rem(me + r, GROUP)
            for a in range(2):
                remote(xl.at[g, a], xl.at[g, a], xs_s.at[r - 1, a], xs_r.at[g, a], core_dev).wait_recv()

    y_select(2)
    ig_multiply()
    xl[me] = land[me]
    y_forward(1)
    y_forward(0)
    x_first(2)
    y_select(1)
    y_select(0)
    ig_first()
    x_forward(2)
    x_last(2)
    x_first(1)
    slices_wait()
    z_first(2)
    x_first(0)
    x_forward(1)
    ig_zsend[...] = ig_sum(0, anti).astype(BF16)
    iz = start(ig_zsend, ig_zland, iz_s, iz_r, anti_dev)
    x_last(1)
    x_forward(0)
    z_first(1)
    rows_first(2)
    x_last(0)
    z_first(0)
    ig_own[...] = ig_sum(1, tp)
    rows_first(1)
    rows_last(2)
    rows_first(0)
    rows_last(1)
    rows_last(0)
    iz.wait_recv()
    ig_out[...] = (ig_own[...] + ig_zland[...].astype(F32)).astype(BF16)

    for cp in sent:
        cp.wait_send()


def adam(ig, grad, master, mom_one, mom_two, ig_out, master_out, one_out, two_out):
    ig_out[...] = ig[...]
    one = beta_one * mom_one[...] + (1.0 - beta_one) * grad[...]
    two = beta_two * mom_two[...] + (1.0 - beta_two) * grad[...] * grad[...]
    update = one / bias_one / (jnp.sqrt(two / bias_two) + adam_eps) + decay_rate * master[...]
    master_out[...] = master[...] - learn_rate * update
    one_out[...] = one
    two_out[...] = two


def per_device(tokens, cotangent, working, degraded, block_map, master, moment_one, moment_two):
    vmem = pl.BlockSpec(memory_space=pltpu.VMEM)
    smem = pl.BlockSpec(memory_space=pltpu.SMEM)
    hbm = pl.BlockSpec(memory_space=pltpu.HBM)
    dma = pltpu.SemaphoreType.DMA
    rows = jax.ShapeDtypeStruct((3, 8, D), F32)
    shard = jax.ShapeDtypeStruct((TOK, SHARD), BF16)
    ig, grad = pl.pallas_call(
        kernel,
        name="swiglu_step",
        out_shape=(shard, rows),
        in_specs=[hbm, hbm, hbm, smem, smem],
        out_specs=(vmem, vmem),
        scratch_shapes=[
            pltpu.VMEM((3, SLOTS * BLOCK, D), BF16),
            pltpu.VMEM((N_TP, 2, TOK, SHARD), BF16),
            pltpu.VMEM((GROUP, 2, TOK, SHARD), BF16),
            pltpu.VMEM((TOK, D), BF16),
            pltpu.VMEM((TOK, D), BF16),
            pltpu.SMEM((BLOCKS,), jnp.int32),
            pltpu.SMEM((SLOTS,), F32),
            pltpu.VMEM((N_Y, 3, UNIT, BLOCK), BF16),
            pltpu.VMEM((3, 2, TOK, BLOCK), BF16),
            pltpu.VMEM((3, 2, TOK, BLOCK), BF16),
            pltpu.VMEM((3, 2, TOK, BLOCK), BF16),
            pltpu.VMEM((GROUP, 3, 2 * BLOCK, TOK), BF16),
            pltpu.VMEM((N_TP, TOK, SHARD), BF16),
            pltpu.VMEM((3, 2, TOK, SHARD), BF16),
            pltpu.VMEM((TOK, SHARD), BF16),
            pltpu.VMEM((TOK, SHARD), BF16),
            pltpu.VMEM((TOK, SHARD), F32),
            pltpu.VMEM((2, TOK, SLOTS * BLOCK), F32),
            pltpu.VMEM((3, N_ZL, 64, SHARD), F32),
            pltpu.VMEM((3, N_ZL, 64, SHARD), BF16),
            pltpu.VMEM((3, 3, 64, SHARD), BF16),
            pltpu.VMEM((3, GROUP, 8, SHARD), F32),
            pltpu.VMEM((3, GROUP, 8, SHARD), F32),
            dma((5,)),
            dma((2, 9)),
            dma((2, 9)),
            dma((7, 2)),
            dma((GROUP, 2)),
            dma((3, 4)),
            dma((3, 4)),
            dma((3,)),
            dma((3,)),
            dma((3, 8)),
            dma((3, 8)),
            dma((3, 2)),
            dma((3, 2)),
            dma,
            dma,
            dma((3, 3)),
            dma((3, 3)),
            dma((3, GROUP - 1)),
            dma((3, GROUP - 1)),
        ],
        compiler_params=pltpu.CompilerParams(
            collective_id=0, has_side_effects=True, vmem_limit_bytes=55 * 1024 * 1024
        ),
        cost_estimate=pl.CostEstimate(flops=3_700_000_000, bytes_accessed=12_000_000, transcendentals=73728),
    )(tokens, cotangent, working.reshape(working.shape[2:]), degraded, block_map)
    return pl.pallas_call(
        adam,
        name="adamw",
        out_shape=(shard, rows, rows, rows),
        in_specs=[vmem] * 5,
        out_specs=(vmem,) * 4,
        compiler_params=pltpu.CompilerParams(vmem_limit_bytes=8 * 1024 * 1024),
    )(ig, grad, master, moment_one, moment_two)


def solution(mesh):
    return jax.shard_map(
        per_device,
        mesh=mesh,
        in_specs=(
            P("dp", "tp"),
            P("dp", "tp"),
            P("dp", "tp", None, None, None),
            P("dp"),
            P("dp", None),
            P(None, ("tp", "dp"), None),
            P(None, ("tp", "dp"), None),
            P(None, ("tp", "dp"), None),
        ),
        out_specs=(
            P("dp", "tp"),
            P(None, ("tp", "dp"), None),
            P(None, ("tp", "dp"), None),
            P(None, ("tp", "dp"), None),
        ),
        check_vma=False,
    )
```

time: 539 us -> 106 us (0.20)
  waiting for transfers between devices: 467 us -> 0 us
  Pallas kernels: 0 us -> 102 us
  matrix products: 22.8 us -> 0 us
  local copies, waits for them, and re-layouts: 22.8 us -> 1.91 us
  between operations: 14.6 us -> 1.43 us
    unnamed x7 -> x0, waiting for transfers between devices: 253 us -> none
    all_gather x3 -> x0, waiting for transfers between devices: 214 us -> none  [the longest x1 83.2 us: per_device(): shard_piece = lax.all_gather(packed, 'tp', axis=0, tiled=True)]
    pallas_call x0 -> x2, Pallas kernels: none -> 102 us  [the longest x1 101 us: per_device(): pl.pallas_call(kernel, name='swiglu_step', out_shape=(shard, rows), in_sp...]
    dot_general x9 -> x0, matrix products: 22.8 us -> none  [the longest x1 4.59 us: per_device(): jnp.einsum('kn,ntc->ktc', selector, shard_piece, preferred_element_type=j...]
    unnamed x17 -> x10, local copies, waits for them, and re-layouts: 14.5 us -> 1.91 us
  transfers between devices with their start and end apart: 5 -> 0, of which waited for: 5 -> 0; matrix products, arithmetic and copies ran while one was open for 6% -> 0% of each run, Pallas kernels for 0% -> 0%
where the time goes in v2:
time: 106 us; the launch traced here: 105 us
  Pallas kernels  102 us (96%)
  local copies, waits for them, and re-layouts  1.91 us (2%)
  between operations  1.43 us (1%)
    pallas_call x1, Pallas kernels, per_device(): pl.pallas_call(kernel, name='swiglu_step', out_shape=(shard, rows), in_sp...  101 us

profile of v2, /device:TPU:25, one launch (start us, length us, event | category | flops | bytes accessed | tf_op | source)
XLA Modules:
  0.0 105.2 jit_solution(4881370852441873612)
XLA Ops:
  0.6 0.0 copy-start.2
  0.6 0.0 copy-start.1
  0.7 0.0 copy-start
  1.4 100.6 %swiglu_step.1 = (bf16[192,448]{1,0:T(8,128)(2,1)}, f32[3,8,3584]{2,1,0:T(8,128)}) custom-call(bf16[192,448]{1,0:T(8,128)(2,1)} %tok.1, bf16[192,448]{1,0:T(8,128)(2,1)} %cot.1, bf16[3,384,3584]{2,1,0:T(8,128)(2,1)} %bitcast.1, s32[1]{0:T(128)S(6)} %copy.12.flag, s32[1,16]{1,0:T(1,128)} %bmap.1), custom_call_target="tpu_custom_call" | custom-call | flops 3700000000 | bytes 12000000 | tf_op jit(solution)/shard_map/swiglu_step/pallas_call | solution.py:398
  102.0 0.0 copy-done.2
  102.0 0.0 copy-done.1
  102.0 0.0 copy-done
  102.0 0.0 copy-start.3
  102.0 1.0 copy-done.3
  103.0 0.0 copy-start.4
  103.0 0.9 copy-done.4
  103.9 1.3 %adamw.1 = (bf16[192,448]{1,0:T(8,128)(2,1)}, f32[3,8,3584]{2,1,0:T(8,128)}, f32[3,8,3584]{2,1,0:T(8,128)}, f32[3,8,3584]{2,1,0:T(8,128)}) custom-call(bf16[192,448]{1,0:T(8,128)(2,1)S(1)} %copy-done.4, f32[3,8,3584]{2,1,0:T(8,128)S(1)} %copy-done.3, f32[3,8,3584]{2,1,0:T(8,128)S(1)} %copy-done, f32[3,8,3584]{2,1,0:T(8,128)S(1)} %copy-done.1, ...), custom_call_target="tpu_custom_call" | custom-call | tf_op jit(solution)/shard_map/adamw/pallas_call | solution.py:453
Async XLA Ops:
  0.6 101.3 %copy-start.2 = (f32[3,8,3584]{2,1,0:T(8,128)S(1)}, f32[3,8,3584]{2,1,0:T(8,128)}, u32[]{:S(2)}) copy-start(f32[3,8,3584]{2,1,0:T(8,128)} %mom_two.1) | copy-start | bytes 1032196
  0.6 101.3 %copy-start.1 = (f32[3,8,3584]{2,1,0:T(8,128)S(1)}, f32[3,8,3584]{2,1,0:T(8,128)}, u32[]{:S(2)}) copy-start(f32[3,8,3584]{2,1,0:T(8,128)} %mom_one.1) | copy-start | bytes 1032196
  0.7 101.3 %copy-start = (f32[3,8,3584]{2,1,0:T(8,128)S(1)}, f32[3,8,3584]{2,1,0:T(8,128)}, u32[]{:S(2)}) copy-start(f32[3,8,3584]{2,1,0:T(8,128)} %master.1) | copy-start | bytes 1032196
  102.0 1.0 copy-start.3
  103.0 0.9 copy-start.4

commit v3 on v2

--- a/solution.py
+++ b/solution.py
@@ -19,7 +19,10 @@
 SHARD = D // N_TP
 GROUP = 2 * N_X
 UNIT = SLOTS * TOK
-EARLY, LATE = (0, TOK // 2), (TOK // 2, TOK // 2)
+PACKED = TOK * SHARD // BLOCK
+EARLY, LATE = (0, PACKED // 2), (PACKED // 2, PACKED // 2)
+Z_ROWS = 64
+Z_PACKED = Z_ROWS * SHARD // BLOCK
 
 beta_one = 0.9
 beta_two = 0.95
@@ -32,10 +35,23 @@
 NT = (((1,), (1,)), ((), ()))
 
 
+def pack(value):
+    half = value.shape[0] // 2
+    tiles = [value[:, t * BLOCK : (t + 1) * BLOCK] for t in range(3)]
+    return jnp.concatenate(tiles + [jnp.concatenate([value[:half, 3 * BLOCK :], value[half:, 3 * BLOCK :]], axis=1)], axis=0)
+
+
+def unpack(value):
+    rows = value.shape[0] * BLOCK // SHARD
+    tiles = [value[t * rows : (t + 1) * rows] for t in range(3)]
+    last = value[3 * rows :]
+    return jnp.concatenate(tiles + [jnp.concatenate([last[:, :64], last[:, 64:]], axis=0)], axis=1)
+
+
 def kernel(
     tok, cot, work, flag, bmap,
     ig_out, grad_out,
-    w, land, xl, xfull, gfull,
+    w, raw, land, xl, xfull, gfull,
     place, fill, ab, own_sel, az_send, az_land, ftb,
     ig_send, ig_land, ig_zsend, ig_zland, ig_own, act_f,
     part, z_send, z_land, tr, gl,
@@ -91,7 +107,7 @@
     for dev in partners:
         pl.semaphore_signal(barrier, inc=1, device_id=dev, device_id_type=MESH)
 
-    own_copies = [pltpu.make_async_copy(ref, land.at[tp, a], w_sem.at[3 + a]) for a, ref in ((0, tok), (1, cot))]
+    own_copies = [pltpu.make_async_copy(ref, raw.at[a], w_sem.at[3 + a]) for a, ref in ((0, tok), (1, cot))]
     for cp in own_copies:
         cp.start()
     w_copies = [pltpu.make_async_copy(work.at[k], w.at[k], w_sem.at[k]) for k in range(3)]
@@ -111,15 +127,16 @@
     for s in range(SLOTS):
         fill[s] = filled[s]
 
-    for cp in own_copies:
-        cp.wait()
+    for a in range(2):
+        own_copies[a].wait()
+        land[tp, a] = pack(raw[a])
     pl.semaphore_wait(barrier, len(partners))
 
     right, left = y_dev(1), y_dev(3)
     yr, yl = lax.rem(y + 1, 4), lax.rem(y + 3, 4)
     p1 = {}
 
-    def send(a, index, chunk, dev, rows=(0, TOK)):
+    def send(a, index, chunk, dev, rows=(0, PACKED)):
         ref = land.at[chunk, a, pl.ds(*rows)]
         p1[a, index] = start(ref, ref, p1_s.at[a, index], p1_r.at[a, index], dev)
 
@@ -185,7 +202,7 @@
         ya[k, 3] = start(ab.at[yr, k, upper], ab.at[yr, k, upper], ya_s.at[k, 3], ya_r.at[k, 3], left)
 
     for j in range(N_TP):
-        xfull[:, j * SHARD : (j + 1) * SHARD] = land[j, 0]
+        xfull[:, j * SHARD : (j + 1) * SHARD] = unpack(land[j, 0])
     w_copies[0].wait()
     w_copies[1].wait()
     zg = lax.dot_general(xfull[...], w[0], NT, preferred_element_type=F32)
@@ -201,7 +218,7 @@
     slices(1, 1)
     core_slice(1)
     for j in range(N_TP):
-        gfull[:, j * SHARD : (j + 1) * SHARD] = land[j, 1]
+        gfull[:, j * SHARD : (j + 1) * SHARD] = unpack(land[j, 1])
     w_copies[2].wait()
     dh = lax.dot_general(gfull[...], w[2], NT, preferred_element_type=F32)
     y_send(1, dh * act_f[0])
@@ -224,8 +241,8 @@
                 jnp.dot(gate_m, w[0, :, cols], preferred_element_type=F32)
                 + jnp.dot(up_m, w[1, :, cols], preferred_element_type=F32)
             ).astype(BF16)
-            ig_send[2 * p] = value[:, :SHARD]
-            ig_send[2 * p + 1] = value[:, SHARD:]
+            ig_send[2 * p] = pack(value[:, :SHARD])
+            ig_send[2 * p + 1] = pack(value[:, SHARD:])
 
     def select(k, owner, i):
         spot = place[owner * 2 + i]
@@ -249,7 +266,7 @@
             own_sel[k, i] = select(k, tp, i)
 
     x_right, x_left = group_dev(x_at(1), c), group_dev(x_at(3), c)
-    top, bottom = pl.ds(0, BLOCK), pl.ds(BLOCK, BLOCK)
+    top, bottom = pl.ds(0, TOK), pl.ds(TOK, TOK)
     xa = {}
 
     def x_send(k, q, ref, dev):
@@ -257,8 +274,10 @@
 
     def x_first(k):
         az[k].wait_recv()
-        for i in range(2):
-            ftb[me, k, i * BLOCK : (i + 1) * BLOCK, :] = (own_sel[k, i] + az_land[k, i]).T
+        block = [(own_sel[k, i] + az_land[k, i]).T for i in range(2)]
+        ftb[me, k, :BLOCK] = block[0][:, :BLOCK]
+        ftb[me, k, BLOCK : 2 * BLOCK] = block[1][:, :BLOCK]
+        ftb[me, k, 2 * BLOCK :] = jnp.concatenate([block[0][:, BLOCK:], block[1][:, BLOCK:]], axis=1)
         x_send(k, 0, ftb.at[me, k], x_right)
         x_send(k, 1, ftb.at[me, k], x_left)
         x_send(k, 4, ftb.at[me, k], core_dev)
@@ -284,12 +303,20 @@
         a = 0 if k < 2 else 1
         total = None
         for g in range(GROUP):
-            term = jnp.dot(ftb[g, k], xl[g, a], preferred_element_type=F32)
+            last = ftb[g, k, 2 * BLOCK :]
+            lhs = jnp.concatenate(
+                [
+                    jnp.concatenate([ftb[g, k, :BLOCK], last[:, :64]], axis=1),
+                    jnp.concatenate([ftb[g, k, BLOCK : 2 * BLOCK], last[:, 64:]], axis=1),
+                ],
+                axis=0,
+            )
+            term = jnp.dot(lhs, unpack(xl[g, a]), preferred_element_type=F32)
             total = term if total is None else total + term
         for zt in range(N_ZL):
-            piece = total[zt * 64 : (zt + 1) * 64]
+            piece = total[zt * Z_ROWS : (zt + 1) * Z_ROWS]
             part[k, zt] = piece
-            z_send[k, zt] = piece.astype(BF16)
+            z_send[k, zt] = pack(piece.astype(BF16))
         for j in (2, 1, 3):
             zz[k, j] = start(
                 z_send.at[k, lax.rem(zl + j, 4)], z_land.at[k, j - 1], z_s.at[k, j - 1], z_r.at[k, j - 1], z_dev(j)
@@ -300,7 +327,8 @@
     def rows_first(k):
         for j in (1, 2, 3):
             zz[k, j].wait_recv()
-        value = (part[k, zl] + z_land[k, 0].astype(F32)) + (z_land[k, 1].astype(F32) + z_land[k, 2].astype(F32))
+        others = z_land[k, 0].astype(F32) + z_land[k, 1].astype(F32) + z_land[k, 2].astype(F32)
+        value = part[k, zl] + unpack(others)
         tr[k] = (value * (1.0 / REPLICAS)).reshape(GROUP, 8, SHARD)
         for r in range(1, GROUP):
             q = lax.rem(seat + r, GROUP)
@@ -372,7 +400,7 @@
     rows_last(1)
     rows_last(0)
     iz.wait_recv()
-    ig_out[...] = (ig_own[...] + ig_zland[...].astype(F32)).astype(BF16)
+    ig_out[...] = unpack((ig_own[...] + ig_zland[...].astype(F32)).astype(BF16))
 
     for cp in sent:
         cp.wait_send()
@@ -403,8 +431,9 @@
         out_specs=(vmem, vmem),
         scratch_shapes=[
             pltpu.VMEM((3, SLOTS * BLOCK, D), BF16),
-            pltpu.VMEM((N_TP, 2, TOK, SHARD), BF16),
-            pltpu.VMEM((GROUP, 2, TOK, SHARD), BF16),
+            pltpu.VMEM((2, TOK, SHARD), BF16),
+            pltpu.VMEM((N_TP, 2, PACKED, BLOCK), BF16),
+            pltpu.VMEM((GROUP, 2, PACKED, BLOCK), BF16),
             pltpu.VMEM((TOK, D), BF16),
             pltpu.VMEM((TOK, D), BF16),
             pltpu.SMEM((BLOCKS,), jnp.int32),
@@ -413,16 +442,16 @@
             pltpu.VMEM((3, 2, TOK, BLOCK), BF16),
             pltpu.VMEM((3, 2, TOK, BLOCK), BF16),
             pltpu.VMEM((3, 2, TOK, BLOCK), BF16),
-            pltpu.VMEM((GROUP, 3, 2 * BLOCK, TOK), BF16),
-            pltpu.VMEM((N_TP, TOK, SHARD), BF16),
-            pltpu.VMEM((3, 2, TOK, SHARD), BF16),
-            pltpu.VMEM((TOK, SHARD), BF16),
-            pltpu.VMEM((TOK, SHARD), BF16),
-            pltpu.VMEM((TOK, SHARD), F32),
+            pltpu.VMEM((GROUP, 3, 3 * BLOCK, BLOCK), BF16),
+            pltpu.VMEM((N_TP, PACKED, BLOCK), BF16),
+            pltpu.VMEM((3, 2, PACKED, BLOCK), BF16),
+            pltpu.VMEM((PACKED, BLOCK), BF16),
+            pltpu.VMEM((PACKED, BLOCK), BF16),
+            pltpu.VMEM((PACKED, BLOCK), F32),
             pltpu.VMEM((2, TOK, SLOTS * BLOCK), F32),
-            pltpu.VMEM((3, N_ZL, 64, SHARD), F32),
-            pltpu.VMEM((3, N_ZL, 64, SHARD), BF16),
-            pltpu.VMEM((3, 3, 64, SHARD), BF16),
+            pltpu.VMEM((3, N_ZL, Z_ROWS, SHARD), F32),
+            pltpu.VMEM((3, N_ZL, Z_PACKED, BLOCK), BF16),
+            pltpu.VMEM((3, 3, Z_PACKED, BLOCK), BF16),
             pltpu.VMEM((3, GROUP, 8, SHARD), F32),
             pltpu.VMEM((3, GROUP, 8, SHARD), F32),
             dma((5,)),
@@ -456,7 +485,7 @@
         out_shape=(shard, rows, rows, rows),
         in_specs=[vmem] * 5,
         out_specs=(vmem,) * 4,
-        compiler_params=pltpu.CompilerParams(vmem_limit_bytes=8 * 1024 * 1024),
+        compiler_params=pltpu.CompilerParams(vmem_limit_bytes=55 * 1024 * 1024),
     )(ig, grad, master, moment_one, moment_two)
 
 

time: 106 us -> 99.1 us (0.935)
  Pallas kernels: 102 us -> 96.1 us
  local copies, waits for them, and re-layouts: 1.91 us -> 0 us
    pallas_call x1, Pallas kernels: 101 us -> 93.4 us  [per_device(): pl.pallas_call(kernel, name='swiglu_step', out_shape=(shard, rows), in_sp...]
    unnamed x10 -> x0, local copies, waits for them, and re-layouts: 1.91 us -> none
    pallas_call x1, Pallas kernels: 1.28 us -> 2.63 us  [per_device(): pl.pallas_call(adam, name='adamw', out_shape=(shard, rows, rows, rows), i...]
where the time goes in v3:
time: 99.1 us; the launch traced here: 97.4 us
  Pallas kernels  96.1 us (97%)
  between operations  1.29 us (1%)
    pallas_call x1, Pallas kernels, per_device(): pl.pallas_call(kernel, name='swiglu_step', out_shape=(shard, rows), in_sp...  93.4 us
    pallas_call x1, Pallas kernels, per_device(): pl.pallas_call(adam, name='adamw', out_shape=(shard, rows, rows, rows), i...  2.63 us

profile of v3, /device:TPU:25, one launch (start us, length us, event | category | flops | bytes accessed | tf_op | source)
XLA Modules:
  0.0 97.4 jit_solution(13421192424655289803)
XLA Ops:
  1.3 93.4 %swiglu_step.1 = (bf16[192,448]{1,0:T(8,128)(2,1)}, f32[3,8,3584]{2,1,0:T(8,128)}) custom-call(bf16[192,448]{1,0:T(8,128)(2,1)} %tok.1, bf16[192,448]{1,0:T(8,128)(2,1)} %cot.1, bf16[3,384,3584]{2,1,0:T(8,128)(2,1)} %bitcast.1, s32[1]{0:T(128)S(6)} %copy.12.flag, s32[1,16]{1,0:T(1,128)} %bmap.1), custom_call_target="tpu_custom_call" | custom-call | flops 3700000000 | bytes 12000000 | tf_op jit(solution)/shard_map/swiglu_step/pallas_call | solution.py:426
  94.7 2.6 %adamw.1 = (bf16[192,448]{1,0:T(8,128)(2,1)}, f32[3,8,3584]{2,1,0:T(8,128)}, f32[3,8,3584]{2,1,0:T(8,128)}, f32[3,8,3584]{2,1,0:T(8,128)}) custom-call(bf16[192,448]{1,0:T(8,128)(2,1)} %get-tuple-element.6.ig, f32[3,8,3584]{2,1,0:T(8,128)} %get-tuple-element.7.grad, f32[3,8,3584]{2,1,0:T(8,128)} %master.1, f32[3,8,3584]{2,1,0:T(8,128)} %mom_one.1, ...), custom_call_target="tpu_custom_call" | custom-call | tf_op jit(solution)/shard_map/adamw/pallas_call | solution.py:482

commit v4 on v3

--- a/solution.py
+++ b/solution.py
@@ -266,7 +266,6 @@
             own_sel[k, i] = select(k, tp, i)
 
     x_right, x_left = group_dev(x_at(1), c), group_dev(x_at(3), c)
-    top, bottom = pl.ds(0, TOK), pl.ds(TOK, TOK)
     xa = {}
 
     def x_send(k, q, ref, dev):
@@ -280,19 +279,17 @@
         ftb[me, k, 2 * BLOCK :] = jnp.concatenate([block[0][:, BLOCK:], block[1][:, BLOCK:]], axis=1)
         x_send(k, 0, ftb.at[me, k], x_right)
         x_send(k, 1, ftb.at[me, k], x_left)
+        x_send(k, 2, ftb.at[me, k], group_dev(x_at(2), c))
         x_send(k, 4, ftb.at[me, k], core_dev)
 
     def x_forward(k):
         xa[k, 0].wait_recv()
-        x_send(k, 2, ftb.at[c * 4 + x_at(3), k, top], x_right)
         x_send(k, 5, ftb.at[c * 4 + x_at(3), k], core_dev)
         xa[k, 1].wait_recv()
-        x_send(k, 3, ftb.at[c * 4 + x_at(1), k, bottom], x_left)
         x_send(k, 6, ftb.at[c * 4 + x_at(1), k], core_dev)
 
     def x_last(k):
         xa[k, 2].wait_recv()
-        xa[k, 3].wait_recv()
         x_send(k, 7, ftb.at[c * 4 + x_at(2), k], core_dev)
 
     zz = {}
@@ -370,31 +367,31 @@
                 remote(xl.at[g, a], xl.at[g, a], xs_s.at[r - 1, a], xs_r.at[g, a], core_dev).wait_recv()
 
     y_select(2)
+    y_forward(1)
     ig_multiply()
     xl[me] = land[me]
-    y_forward(1)
     y_forward(0)
     x_first(2)
     y_select(1)
     y_select(0)
+    x_forward(2)
+    x_first(1)
+    x_last(2)
     ig_first()
-    x_forward(2)
-    x_last(2)
-    x_first(1)
+    x_first(0)
     slices_wait()
     z_first(2)
-    x_first(0)
     x_forward(1)
-    ig_zsend[...] = ig_sum(0, anti).astype(BF16)
-    iz = start(ig_zsend, ig_zland, iz_s, iz_r, anti_dev)
     x_last(1)
+    z_first(1)
     x_forward(0)
-    z_first(1)
     rows_first(2)
     x_last(0)
     z_first(0)
+    ig_zsend[...] = ig_sum(0, anti).astype(BF16)
+    iz = start(ig_zsend, ig_zland, iz_s, iz_r, anti_dev)
+    rows_first(1)
     ig_own[...] = ig_sum(1, tp)
-    rows_first(1)
     rows_last(2)
     rows_first(0)
     rows_last(1)

time: 99.1 us -> 96.6 us (0.975)
  Pallas kernels: 96.1 us -> 93.5 us
    pallas_call x1, Pallas kernels: 93.4 us -> 90.9 us  [per_device(): pl.pallas_call(kernel, name='swiglu_step', out_shape=(shard, rows), in_sp...]
where the time goes in v4:
time: 96.6 us; the launch traced here: 94.8 us
  Pallas kernels  93.5 us (97%)
  between operations  1.29 us (1%)
    pallas_call x1, Pallas kernels, per_device(): pl.pallas_call(kernel, name='swiglu_step', out_shape=(shard, rows), in_sp...  90.9 us
    pallas_call x1, Pallas kernels, per_device(): pl.pallas_call(adam, name='adamw', out_shape=(shard, rows, rows, rows), i...  2.63 us

profile of v4, /device:TPU:25, one launch (start us, length us, event | category | flops | bytes accessed | tf_op | source)
XLA Modules:
  0.0 94.8 jit_solution(17370879876424049286)
XLA Ops:
  1.3 90.9 %swiglu_step.1 = (bf16[192,448]{1,0:T(8,128)(2,1)}, f32[3,8,3584]{2,1,0:T(8,128)}) custom-call(bf16[192,448]{1,0:T(8,128)(2,1)} %tok.1, bf16[192,448]{1,0:T(8,128)(2,1)} %cot.1, bf16[3,384,3584]{2,1,0:T(8,128)(2,1)} %bitcast.1, s32[1]{0:T(128)S(6)} %copy.12.flag, s32[1,16]{1,0:T(1,128)} %bmap.1), custom_call_target="tpu_custom_call" | custom-call | flops 3700000000 | bytes 12000000 | tf_op jit(solution)/shard_map/swiglu_step/pallas_call | solution.py:423
  92.2 2.6 %adamw.1 = (bf16[192,448]{1,0:T(8,128)(2,1)}, f32[3,8,3584]{2,1,0:T(8,128)}, f32[3,8,3584]{2,1,0:T(8,128)}, f32[3,8,3584]{2,1,0:T(8,128)}) custom-call(bf16[192,448]{1,0:T(8,128)(2,1)} %get-tuple-element.6.ig, f32[3,8,3584]{2,1,0:T(8,128)} %get-tuple-element.7.grad, f32[3,8,3584]{2,1,0:T(8,128)} %master.1, f32[3,8,3584]{2,1,0:T(8,128)} %mom_one.1, ...), custom_call_target="tpu_custom_call" | custom-call | tf_op jit(solution)/shard_map/adamw/pallas_call | solution.py:479

commit v5 on v4

--- a/solution.py
+++ b/solution.py
@@ -420,6 +420,8 @@
     dma = pltpu.SemaphoreType.DMA
     rows = jax.ShapeDtypeStruct((3, 8, D), F32)
     shard = jax.ShapeDtypeStruct((TOK, SHARD), BF16)
+    whole = pl.BlockSpec((TOK, SHARD), lambda k: (0, 0))
+    third = pl.BlockSpec((1, 8, D), lambda k: (k, 0, 0))
     ig, grad = pl.pallas_call(
         kernel,
         name="swiglu_step",
@@ -480,8 +482,9 @@
         adam,
         name="adamw",
         out_shape=(shard, rows, rows, rows),
-        in_specs=[vmem] * 5,
-        out_specs=(vmem,) * 4,
+        grid=(3,),
+        in_specs=[whole] + [third] * 4,
+        out_specs=(whole,) + (third,) * 3,
         compiler_params=pltpu.CompilerParams(vmem_limit_bytes=55 * 1024 * 1024),
     )(ig, grad, master, moment_one, moment_two)
 

time: 96.6 us -> 97.5 us (level)
  no operation moved by 1% of the time
where the time goes in v5:
time: 97.5 us; the launch traced here: 95.7 us
  Pallas kernels  94.4 us (97%)
  between operations  1.29 us (1%)
    pallas_call x1, Pallas kernels, per_device(): pl.pallas_call(kernel, name='swiglu_step', out_shape=(shard, rows), in_sp...  90.9 us
    pallas_call x1, Pallas kernels, per_device(): pl.pallas_call(adam, name='adamw', out_shape=(shard, rows, rows, rows), g...  3.53 us

profile of v5, /device:TPU:25, one launch (start us, length us, event | category | flops | bytes accessed | tf_op | source)
XLA Modules:
  0.0 95.7 jit_solution(10437912603821204290)
XLA Ops:
  1.3 90.9 %swiglu_step.1 = (bf16[192,448]{1,0:T(8,128)(2,1)}, f32[3,8,3584]{2,1,0:T(8,128)}) custom-call(bf16[192,448]{1,0:T(8,128)(2,1)} %tok.1, bf16[192,448]{1,0:T(8,128)(2,1)} %cot.1, bf16[3,384,3584]{2,1,0:T(8,128)(2,1)} %bitcast.1, s32[1]{0:T(128)S(6)} %copy.12.flag, s32[1,16]{1,0:T(1,128)} %bmap.1), custom_call_target="tpu_custom_call" | custom-call | flops 3700000000 | bytes 12000000 | tf_op jit(solution)/shard_map/swiglu_step/pallas_call | solution.py:425
  92.2 3.5 %adamw.1 = (bf16[192,448]{1,0:T(8,128)(2,1)}, f32[3,8,3584]{2,1,0:T(8,128)}, f32[3,8,3584]{2,1,0:T(8,128)}, f32[3,8,3584]{2,1,0:T(8,128)}) custom-call(bf16[192,448]{1,0:T(8,128)(2,1)} %get-tuple-element.6.ig, f32[3,8,3584]{2,1,0:T(8,128)} %get-tuple-element.7.grad, f32[3,8,3584]{2,1,0:T(8,128)} %master.1, f32[3,8,3584]{2,1,0:T(8,128)} %mom_one.1, ...), custom_call_target="tpu_custom_call" | custom-call | tf_op jit(solution)/shard_map/adamw/pallas_call | solution.py:481
